TPU v7x, 32 devices: a whole 2x2x4 slice. The times are simulated.
32 devices in a mesh: trial: 2 (over x), wide: 8 (over z, y), narrow: 2 (over core).
Axes of the slice: x: 2, y: 2, z: 4, core: 2. Of those that a mesh axis runs over, the one named last changes fastest.
Arguments:
- points: float32 [32, 32768], P(None, ('trial', 'wide', 'narrow')), parts along dimension 1, may hold values from -6 to 6
- probes: bfloat16 [17, 32768], P(None, ('trial', 'wide', 'narrow')), parts along dimension 1, may hold values from -6 to 6
- lengthscale: float32 [64], P('trial'), parts along dimension 0, may hold values from 1.5 to 4
- noise: float32 [2], P('trial'), parts along dimension 0, may hold values from 0.3 to 1.5
Outputs:
- product: float32 [17, 32768], P(None, ('trial', 'wide', 'narrow')), parts along dimension 1
There are 2 independent parts, one for each index of `trial`. A program takes and returns all parts, laid end to end along the dimension named above; each array names one. Nothing has to cross between parts.
All inputs are finite; a program needn't handle non-finite values.
Results may differ from a plain program's by a relative error of at most 0.0046.
Values may be sent and summed in bfloat16 or wider, within the bound.
A program may use at most 64 MiB of HBM per device.

v0:
```python
import jax
import jax.numpy as jnp
from jax import lax
from jax.sharding import PartitionSpec as P


def passed_along(block, axis, distance):
    devices = range(lax.axis_size(axis))
    route = [((i - distance) % len(devices), i) for i in devices]
    return lax.ppermute(block, axis, route)


def kernel_tile(rows_x, rows_n, cols_x):
    cols_f = cols_x.astype(jnp.float32)
    cols_n = jnp.sum(cols_f * cols_f, axis=0)
    cross = lax.dot_general(
        rows_x, cols_x, (((0,), (0,)), ((), ())), preferred_element_type=jnp.float32
    )
    return jnp.exp(-0.5 * (rows_n[:, None] + cols_n[None, :] - 2.0 * cross)).astype(jnp.bfloat16)


def row_term(tile, cols_v):
    return lax.dot_general(
        cols_v, tile, (((1,), (1,)), ((), ())), preferred_element_type=jnp.float32
    )


def col_term(tile, rows_v):
    return lax.dot_general(
        rows_v, tile, (((1,), (0,)), ((), ())), preferred_element_type=jnp.float32
    )


def body(points, probes, lengthscale, noise):
    scaled = (points / lengthscale[:, None]).astype(jnp.bfloat16)
    super_x, super_v = (
        lax.all_gather(scaled, "narrow", axis=1, tiled=True),
        lax.all_gather(probes, "narrow", axis=1, tiled=True),
    )
    super_f = super_x.astype(jnp.float32)
    super_n = jnp.sum(super_f * super_f, axis=0)
    loop_len = lax.axis_size("wide")
    half_len = loop_len // 2
    total = row_term(kernel_tile(super_x, super_n, scaled), probes)
    extra = jnp.zeros(probes.shape, jnp.float32)

    def advance(visit_x, visit_v):
        return passed_along((visit_x, visit_v), "wide", 1)

    def two_sided(step, carry):
        visit_x, visit_v, riders, sums = carry
        visit_x, visit_v = advance(visit_x, visit_v)
        riders = passed_along(riders, "wide", 1)
        tile = kernel_tile(super_x, super_n, visit_x)
        return (visit_x, visit_v, riders + col_term(tile, super_v), sums + row_term(tile, visit_v))

    visit_x, visit_v, riders, total = lax.fori_loop(
        1, half_len, two_sided, (scaled, probes, extra, total)
    )
    visit_x, visit_v = advance(visit_x, visit_v)
    total = total + row_term(kernel_tile(super_x, super_n, visit_x), visit_v)
    extra = passed_along(riders, "wide", half_len + 1)
    summed = lax.psum_scatter(total, "narrow", scatter_dimension=1, tiled=True)
    return summed + extra + noise[0] * probes.astype(jnp.float32)


def solution(mesh):
    placed = (
        P(None, ("trial", "wide", "narrow")),
        P(None, ("trial", "wide", "narrow")),
        P("trial"),
        P("trial"),
    )
    return jax.shard_map(
        body,
        mesh=mesh,
        in_specs=placed,
        out_specs=P(None, ("trial", "wide", "narrow")),
        check_vma=False,
    )
```

profile of v0, /device:TPU:0, one launch (start us, length us, event | category | flops | bytes accessed | tf_op | source)
XLA Modules:
  0.0 78.3 jit_solution(10830385861049388460)
XLA Ops:
  6.5 2.3 %all_gather.7 = bf16[17,2048]{1,0:T(8,128)(2,1)S(1)} all-gather(bf16[17,1024]{1,0:T(8,128)(2,1)} %param.7), channel_id=1, replica_groups=mesh['trial'=2,'wide'=8,'narrow'=2] {'narrow'}, dimensions={1}, use_global_device_ids=true | all-gather | bytes 104448 | tf_op jit(solution)/shard_map/all_gather | solution.py:38
  8.9 1.0 %multiply_reduce_fusion.3 = (f32[1024]{0:T(1024)S(1)}, bf16[32,1024]{1,0:T(8,128)(2,1)S(1)}) fusion(f32[32,1024]{1,0:T(8,128)} %param.6, f32[32]{0:T(128)} %param.8), kind=kLoop, calls=%fused_computation.13 | loop fusion | flops 162816 | bytes 200832 | tf_op jit(solution)/shard_map/reduce_sum | solution.py:15
  9.9 1.9 %all_gather.6 = bf16[32,2048]{1,0:T(8,128)(2,1)S(1)} all-gather(bf16[32,1024]{1,0:T(8,128)(2,1)S(1)} %get-tuple-element.149), channel_id=1, replica_groups=mesh['trial'=2,'wide'=8,'narrow'=2] {'narrow'}, dimensions={1}, use_global_device_ids=true | all-gather | bytes 196608 | tf_op jit(solution)/shard_map/all_gather | solution.py:37
  11.9 3.6 %convolution_bitcast_fusion.2 = f32[17,2048]{1,0:T(8,128)S(1)} fusion(bf16[17,1024]{1,0:T(8,128)(2,1)} %param.7, bf16[32,2048]{1,0:T(8,128)(2,1)S(1)} %all_gather.6, bf16[32,1024]{1,0:T(8,128)(2,1)S(1)} %get-tuple-element.149, f32[1024]{0:T(1024)S(1)} %get-tuple-element.97, f32[2048]{0:T(1024)S(1)} %multiply_reduce_fusion.1), kind=kOutput, calls=%fused_computation.9 | convolution fusion | flops 216006656 | bytes 382976 | tf_op jit(solution)/shard_map/dot_general | solution.py:23
  15.5 37.7 %while.17 = (s32[]{:T(128)}, bf16[32,1024]{1,0:T(8,128)(2,1)S(1)}, bf16[17,1024]{1,0:T(8,128)(2,1)S(1)}, f32[17,1024]{1,0:T(8,128)S(1)}, f32[17,2048]{1,0:T(8,12...) while((s32[]{:T(128)}, bf16[32,1024]{1,0:T(8,128)(2,1)S(1)}, ...), condition=%wide.region_4.0_spmd.clone, body=%wide.region_2.0_spmd.clone.sunk | while | flops 287476736 | bytes 14403815 | solution.py:57
  15.5 2.9 %collective-permute-start = (bf16[32,1024]{1,0:T(8,128)(2,1)S(1)}, bf16[32,1024]{1,0:T(8,128)(2,1)S(1)}, u32[]{:S(2)}, u32[]{:S(2)}) collective-permute-start(bf16[32,1024]{1,0:T(8,128)(2,1)S(1)} %get-tuple-element.159), channel_id=1, source_target_pairs={{14,0},{0,2},{2,4},{4,6},{6,8},{8,10},{10,12},{12,14},{15,1},{1,3}... | collective-permute-start | bytes 196616 | tf_op jit(solution)/shard_map/while/body/eval_jaxpr/ppermute | solution.py:10
  18.4 1.5 %collective-permute-start.1 = (bf16[17,1024]{1,0:T(8,128)(2,1)S(1)}, bf16[17,1024]{1,0:T(8,128)(2,1)S(1)}, u32[]{:S(2)}, u32[]{:S(2)}) collective-permute-start(bf16[17,1024]{1,0:T(8,128)(2,1)S(1)} %get-tuple-element.160), channel_id=1, source_target_pairs={{14,0},{0,2},{2,4},{4,6},{6,8},{8,10},{10,12},{12,14},{15,1},{1,3}... | collective-permute-start | bytes 104456 | tf_op jit(solution)/shard_map/while/body/eval_jaxpr/ppermute | solution.py:10
  19.9 1.6 %collective-permute-start.2 = (f32[17,1024]{1,0:T(8,128)S(1)}, f32[17,1024]{1,0:T(8,128)S(1)}, u32[]{:S(2)}, u32[]{:S(2)}) collective-permute-start(f32[17,1024]{1,0:T(8,128)S(1)} %broadcast_select_fusion.2), channel_id=1, source_target_pairs={{14,0},{0,2},{2,4},{4,6},{6,8},{8,10},{10,12},{12,14},{15,1},{1,3}... | collective-permute-start | bytes 208904 | tf_op jit(solution)/shard_map/while/body/eval_jaxpr/ppermute | solution.py:10
  21.5 4.0 %collective-permute-done.1 = bf16[17,1024]{1,0:T(8,128)(2,1)S(1)} collective-permute-done((bf16[17,1024]{1,0:T(8,128)(2,1)S(1)}, bf16[17,1024]{1,0:T(8,128)(2,1)S(1)}, u32[]{:S(2)}, u32[]{:S(2)}) %collective-permute-start.1) | collective-permute-done | bytes 34848 | tf_op jit(solution)/shard_map/while/body/eval_jaxpr/ppermute | solution.py:10
  25.5 2.2 %exponential_convert_fusion.4 = bf16[2048,1024]{1,0:T(8,128)(2,1)S(1)} fusion(bf16[32,2048]{1,0:T(8,128)(2,1)S(1)} %get-tuple-element.174, bf16[32,1024]{1,0:T(8,128)(2,1)S(1)} %collective-permute-done, f32[1024]{0:T(1024)S(1)} %multiply_reduce_fusion.5, f32[2048]{0:T(1024)S(1)} %get-tuple-element.173), kind=kOutput, calls=%fused_computation.clone.1 | convolution fusion | flops 144703488 | bytes 4403200 | tf_op jit(solution)/shard_map/while/body/eval_jaxpr/dot_general | solution.py:16
  27.7 1.2 %fusion.33 = f32[17,2048]{1,0:T(8,128)S(1)} fusion(f32[17,2048]{1,0:T(8,128)S(1)} %get-tuple-element.162, bf16[2048,1024]{1,0:T(8,128)(2,1)S(1)} %exponential_convert_fusion.4, bf16[17,1024]{1,0:T(8,128)(2,1)S(1)} %collective-permute-done.1), kind=kOutput, calls=%fused_computation.2.clone.1 | convolution fusion | flops 71337984 | bytes 4507648 | tf_op jit(solution)/shard_map/while/body/eval_jaxpr/dot_general | solution.py:23
  29.0 0.7 fusion.32
  29.7 1.2 %collective-permute-start.1 = (bf16[17,1024]{1,0:T(8,128)(2,1)S(1)}, bf16[17,1024]{1,0:T(8,128)(2,1)S(1)}, u32[]{:S(2)}, u32[]{:S(2)}) collective-permute-start(bf16[17,1024]{1,0:T(8,128)(2,1)S(1)} %get-tuple-element.160), channel_id=1, source_target_pairs={{14,0},{0,2},{2,4},{4,6},{6,8},{8,10},{10,12},{12,14},{15,1},{1,3}... | collective-permute-start | bytes 104456 | tf_op jit(solution)/shard_map/while/body/eval_jaxpr/ppermute | solution.py:10
  30.9 0.7 collective-permute-start.2
  31.6 5.7 %collective-permute-done.1 = bf16[17,1024]{1,0:T(8,128)(2,1)S(1)} collective-permute-done((bf16[17,1024]{1,0:T(8,128)(2,1)S(1)}, bf16[17,1024]{1,0:T(8,128)(2,1)S(1)}, u32[]{:S(2)}, u32[]{:S(2)}) %collective-permute-start.1) | collective-permute-done | bytes 34848 | tf_op jit(solution)/shard_map/while/body/eval_jaxpr/ppermute | solution.py:10
  37.3 2.2 %exponential_convert_fusion.4 = bf16[2048,1024]{1,0:T(8,128)(2,1)S(1)} fusion(bf16[32,2048]{1,0:T(8,128)(2,1)S(1)} %get-tuple-element.174, bf16[32,1024]{1,0:T(8,128)(2,1)S(1)} %collective-permute-done, f32[1024]{0:T(1024)S(1)} %multiply_reduce_fusion.5, f32[2048]{0:T(1024)S(1)} %get-tuple-element.173), kind=kOutput, calls=%fused_computation.clone.1 | convolution fusion | flops 144703488 | bytes 4403200 | tf_op jit(solution)/shard_map/while/body/eval_jaxpr/dot_general | solution.py:16
  39.5 1.2 %fusion.33 = f32[17,2048]{1,0:T(8,128)S(1)} fusion(f32[17,2048]{1,0:T(8,128)S(1)} %get-tuple-element.162, bf16[2048,1024]{1,0:T(8,128)(2,1)S(1)} %exponential_convert_fusion.4, bf16[17,1024]{1,0:T(8,128)(2,1)S(1)} %collective-permute-done.1), kind=kOutput, calls=%fused_computation.2.clone.1 | convolution fusion | flops 71337984 | bytes 4507648 | tf_op jit(solution)/shard_map/while/body/eval_jaxpr/dot_general | solution.py:23
  40.8 0.7 fusion.32
  41.5 0.2 collective-permute-start.1
  41.7 0.6 collective-permute-start.2
  42.3 6.7 %collective-permute-done.1 = bf16[17,1024]{1,0:T(8,128)(2,1)S(1)} collective-permute-done((bf16[17,1024]{1,0:T(8,128)(2,1)S(1)}, bf16[17,1024]{1,0:T(8,128)(2,1)S(1)}, u32[]{:S(2)}, u32[]{:S(2)}) %collective-permute-start.1) | collective-permute-done | bytes 34848 | tf_op jit(solution)/shard_map/while/body/eval_jaxpr/ppermute | solution.py:10
  49.0 2.2 %exponential_convert_fusion.4 = bf16[2048,1024]{1,0:T(8,128)(2,1)S(1)} fusion(bf16[32,2048]{1,0:T(8,128)(2,1)S(1)} %get-tuple-element.174, bf16[32,1024]{1,0:T(8,128)(2,1)S(1)} %collective-permute-done, f32[1024]{0:T(1024)S(1)} %multiply_reduce_fusion.5, f32[2048]{0:T(1024)S(1)} %get-tuple-element.173), kind=kOutput, calls=%fused_computation.clone.1 | convolution fusion | flops 144703488 | bytes 4403200 | tf_op jit(solution)/shard_map/while/body/eval_jaxpr/dot_general | solution.py:16
  51.2 1.2 %fusion.33 = f32[17,2048]{1,0:T(8,128)S(1)} fusion(f32[17,2048]{1,0:T(8,128)S(1)} %get-tuple-element.162, bf16[2048,1024]{1,0:T(8,128)(2,1)S(1)} %exponential_convert_fusion.4, bf16[17,1024]{1,0:T(8,128)(2,1)S(1)} %collective-permute-done.1), kind=kOutput, calls=%fused_computation.2.clone.1 | convolution fusion | flops 71337984 | bytes 4507648 | tf_op jit(solution)/shard_map/while/body/eval_jaxpr/dot_general | solution.py:23
  52.5 0.7 fusion.32
  53.2 0.1 collective-permute-start.3
  53.3 6.9 %collective-permute-done.4 = bf16[32,1024]{1,0:T(8,128)(2,1)S(1)} collective-permute-done((bf16[32,1024]{1,0:T(8,128)(2,1)S(1)}, bf16[32,1024]{1,0:T(8,128)(2,1)S(1)}, u32[]{:S(2)}, u32[]{:S(2)}) %collective-permute-start.4) | collective-permute-done | bytes 65568 | tf_op jit(solution)/shard_map/ppermute | solution.py:10
  60.2 0.5 collective-permute-done.3
  60.7 3.4 %convolution_add_fusion = f32[17,2048]{1,0:T(8,128)} fusion(f32[17,2048]{1,0:T(8,128)S(1)} %get-tuple-element.50, bf16[17,1024]{1,0:T(8,128)(2,1)S(1)} %collective-permute-done.3, bf16[32,2048]{1,0:T(8,128)(2,1)S(1)} %get-tuple-element.184, bf16[32,1024]{1,0:T(8,128)(2,1)S(1)} %collective-permute-done.4, f32[1024]{0:T(1024)S(1)} %multiply_reduce_fusion.2, ...), kind=kOutput, calls=%fused_computation.10 | convolution fusion | flops 216041472 | bytes 522240 | tf_op jit(solution)/shard_map/dot_general | solution.py:23
  64.1 0.1 collective-permute-start.5
  64.9 4.9 %collective-permute-done.5 = f32[17,1024]{1,0:T(8,128)S(1)} collective-permute-done((f32[17,1024]{1,0:T(8,128)S(1)}, f32[17,1024]{1,0:T(8,128)S(1)}, u32[]{:S(2)}, u32[]{:S(2)}) %collective-permute-start.5) | collective-permute-done | bytes 69664 | tf_op jit(solution)/shard_map/ppermute | solution.py:10
  69.7 0.2 reduce-scatter.2.cloned.1.call-done
  69.9 1.5 %multiply_add_fusion = f32[17,1024]{1,0:T(8,128)} fusion(bf16[17,1024]{1,0:T(8,128)(2,1)S(1)} %copy-done, f32[17,1024]{1,0:T(8,128)} %reduce-scatter.2.cloned.1.call-done, f32[17,1024]{1,0:T(8,128)S(1)} %collective-permute-done.5, f32[]{:T(128)} %bitcast.39), kind=kLoop, calls=%fused_computation.15 | loop fusion | flops 69632 | bytes 243716 | tf_op jit(solution)/shard_map/add | solution.py:64
  (30 shorter events, 0.4 us)
Async XLA Ops:
  6.5 63.4 %reduce-scatter.2.cloned.1.call-start = ((), (), s32[]{:S(2)}) async-start(), calls=%async_computation.1 | async-start | bytes 294912 | tf_op jit(solution)/shard_map/reduce_scatter | solution.py:63
  11.8 3.6 %copy-start.1 = (bf16[17,1024]{1,0:T(8,128)(2,1)S(1)}, bf16[17,1024]{1,0:T(8,128)(2,1)}, u32[]{:S(2)}) copy-start(bf16[17,1024]{1,0:T(8,128)(2,1)} %param.7) | copy-start | bytes 104452
  15.5 10.0 %collective-permute-start = (bf16[32,1024]{1,0:T(8,128)(2,1)S(1)}, bf16[32,1024]{1,0:T(8,128)(2,1)S(1)}, u32[]{:S(2)}, u32[]{:S(2)}) collective-permute-start(bf16[32,1024]{1,0:T(8,128)(2,1)S(1)} %get-tuple-element.159), channel_id=1, source_target_pairs={{14,0},{0,2},{2,4},{4,6},{6,8},{8,10},{10,12},{12,14},{15,1},{1,3}... | collective-permute-start | bytes 196616 | tf_op jit(solution)/shard_map/while/body/eval_jaxpr/ppermute | solution.py:10
  18.4 7.1 %collective-permute-start.1 = (bf16[17,1024]{1,0:T(8,128)(2,1)S(1)}, bf16[17,1024]{1,0:T(8,128)(2,1)S(1)}, u32[]{:S(2)}, u32[]{:S(2)}) collective-permute-start(bf16[17,1024]{1,0:T(8,128)(2,1)S(1)} %get-tuple-element.160), channel_id=1, source_target_pairs={{14,0},{0,2},{2,4},{4,6},{6,8},{8,10},{10,12},{12,14},{15,1},{1,3}... | collective-permute-start | bytes 104456 | tf_op jit(solution)/shard_map/while/body/eval_jaxpr/ppermute | solution.py:10
  19.9 9.0 %collective-permute-start.2 = (f32[17,1024]{1,0:T(8,128)S(1)}, f32[17,1024]{1,0:T(8,128)S(1)}, u32[]{:S(2)}, u32[]{:S(2)}) collective-permute-start(f32[17,1024]{1,0:T(8,128)S(1)} %broadcast_select_fusion.2), channel_id=1, source_target_pairs={{14,0},{0,2},{2,4},{4,6},{6,8},{8,10},{10,12},{12,14},{15,1},{1,3}... | collective-permute-start | bytes 208904 | tf_op jit(solution)/shard_map/while/body/eval_jaxpr/ppermute | solution.py:10
  29.6 7.7 %collective-permute-start = (bf16[32,1024]{1,0:T(8,128)(2,1)S(1)}, bf16[32,1024]{1,0:T(8,128)(2,1)S(1)}, u32[]{:S(2)}, u32[]{:S(2)}) collective-permute-start(bf16[32,1024]{1,0:T(8,128)(2,1)S(1)} %get-tuple-element.159), channel_id=1, source_target_pairs={{14,0},{0,2},{2,4},{4,6},{6,8},{8,10},{10,12},{12,14},{15,1},{1,3}... | collective-permute-start | bytes 196616 | tf_op jit(solution)/shard_map/while/body/eval_jaxpr/ppermute | solution.py:10
  29.7 7.6 %collective-permute-start.1 = (bf16[17,1024]{1,0:T(8,128)(2,1)S(1)}, bf16[17,1024]{1,0:T(8,128)(2,1)S(1)}, u32[]{:S(2)}, u32[]{:S(2)}) collective-permute-start(bf16[17,1024]{1,0:T(8,128)(2,1)S(1)} %get-tuple-element.160), channel_id=1, source_target_pairs={{14,0},{0,2},{2,4},{4,6},{6,8},{8,10},{10,12},{12,14},{15,1},{1,3}... | collective-permute-start | bytes 104456 | tf_op jit(solution)/shard_map/while/body/eval_jaxpr/ppermute | solution.py:10
  30.9 9.9 %collective-permute-start.2 = (f32[17,1024]{1,0:T(8,128)S(1)}, f32[17,1024]{1,0:T(8,128)S(1)}, u32[]{:S(2)}, u32[]{:S(2)}) collective-permute-start(f32[17,1024]{1,0:T(8,128)S(1)} %broadcast_select_fusion.2), channel_id=1, source_target_pairs={{14,0},{0,2},{2,4},{4,6},{6,8},{8,10},{10,12},{12,14},{15,1},{1,3}... | collective-permute-start | bytes 208904 | tf_op jit(solution)/shard_map/while/body/eval_jaxpr/ppermute | solution.py:10
  41.4 7.5 %collective-permute-start = (bf16[32,1024]{1,0:T(8,128)(2,1)S(1)}, bf16[32,1024]{1,0:T(8,128)(2,1)S(1)}, u32[]{:S(2)}, u32[]{:S(2)}) collective-permute-start(bf16[32,1024]{1,0:T(8,128)(2,1)S(1)} %get-tuple-element.159), channel_id=1, source_target_pairs={{14,0},{0,2},{2,4},{4,6},{6,8},{8,10},{10,12},{12,14},{15,1},{1,3}... | collective-permute-start | bytes 196616 | tf_op jit(solution)/shard_map/while/body/eval_jaxpr/ppermute | solution.py:10
  41.5 7.5 %collective-permute-start.1 = (bf16[17,1024]{1,0:T(8,128)(2,1)S(1)}, bf16[17,1024]{1,0:T(8,128)(2,1)S(1)}, u32[]{:S(2)}, u32[]{:S(2)}) collective-permute-start(bf16[17,1024]{1,0:T(8,128)(2,1)S(1)} %get-tuple-element.160), channel_id=1, source_target_pairs={{14,0},{0,2},{2,4},{4,6},{6,8},{8,10},{10,12},{12,14},{15,1},{1,3}... | collective-permute-start | bytes 104456 | tf_op jit(solution)/shard_map/while/body/eval_jaxpr/ppermute | solution.py:10
  41.7 10.7 %collective-permute-start.2 = (f32[17,1024]{1,0:T(8,128)S(1)}, f32[17,1024]{1,0:T(8,128)S(1)}, u32[]{:S(2)}, u32[]{:S(2)}) collective-permute-start(f32[17,1024]{1,0:T(8,128)S(1)} %broadcast_select_fusion.2), channel_id=1, source_target_pairs={{14,0},{0,2},{2,4},{4,6},{6,8},{8,10},{10,12},{12,14},{15,1},{1,3}... | collective-permute-start | bytes 208904 | tf_op jit(solution)/shard_map/while/body/eval_jaxpr/ppermute | solution.py:10
  53.1 7.0 %collective-permute-start.4 = (bf16[32,1024]{1,0:T(8,128)(2,1)S(1)}, bf16[32,1024]{1,0:T(8,128)(2,1)S(1)}, u32[]{:S(2)}, u32[]{:S(2)}) collective-permute-start(bf16[32,1024]{1,0:T(8,128)(2,1)S(1)} %get-tuple-element.52), channel_id=1, source_target_pairs={{14,0},{0,2},{2,4},{4,6},{6,8},{8,10},{10,12},{12,14},{15,1},{1,3}... | collective-permute-start | bytes 196616 | tf_op jit(solution)/shard_map/ppermute | solution.py:10
  53.2 7.5 %collective-permute-start.3 = (bf16[17,1024]{1,0:T(8,128)(2,1)S(1)}, bf16[17,1024]{1,0:T(8,128)(2,1)S(1)}, u32[]{:S(2)}, u32[]{:S(2)}) collective-permute-start(bf16[17,1024]{1,0:T(8,128)(2,1)S(1)} %get-tuple-element.51), channel_id=1, source_target_pairs={{14,0},{0,2},{2,4},{4,6},{6,8},{8,10},{10,12},{12,14},{15,1},{1,3}... | collective-permute-start | bytes 104456 | tf_op jit(solution)/shard_map/ppermute | solution.py:10
  60.7 9.2 %copy-start = (bf16[17,1024]{1,0:T(8,128)(2,1)S(1)}, bf16[17,1024]{1,0:T(8,128)(2,1)}, u32[]{:S(2)}) copy-start(bf16[17,1024]{1,0:T(8,128)(2,1)} %param.7) | copy-start | bytes 104452
  64.1 5.6 %collective-permute-start.5 = (f32[17,1024]{1,0:T(8,128)S(1)}, f32[17,1024]{1,0:T(8,128)S(1)}, u32[]{:S(2)}, u32[]{:S(2)}) collective-permute-start(f32[17,1024]{1,0:T(8,128)S(1)} %get-tuple-element.53), channel_id=1, source_target_pairs={{6,0},{8,2},{10,4},{12,6},{14,8},{0,10},{2,12},{4,14},{7,1},{9,3},... | collective-permute-start | bytes 208904 | tf_op jit(solution)/shard_map/ppermute | solution.py:10
Sparse Core Ops, SparseCore 0:
  64.3 5.6 reduce-scatter.1
where the time goes:
time: 78.5 us; the launch traced here: 78.3 us
  waiting for transfers between devices  28.8 us (37%)
  matrix products  19.2 us (24%)
  between operations  14.1 us (18%)
  starting transfers between devices  8.97 us (11%)
  blocking collectives  4.25 us (5%)
  other arithmetic  2.72 us (3%)
    ppermute x12, waiting for transfers between devices, passed_along(): return lax.ppermute(block, axis, route)  28.6 us
    dot_general x5, matrix products, row_term(): lax.dot_general(cols_v, tile, (((1,), (1,)), ((), ())), preferred_element...  10.7 us
    ppermute x12, starting transfers between devices, passed_along(): return lax.ppermute(block, axis, route)  8.96 us
    dot_general x3, matrix products, kernel_tile(): lax.dot_general(rows_x, cols_x, (((0,), (0,)), ((), ())), preferred_eleme...  6.6 us
    all_gather x1, blocking collectives, body(): lax.all_gather(probes, 'narrow', axis=1, tiled=True)  2.34 us
    dot_general x3, matrix products, col_term(): lax.dot_general(rows_v, tile, (((1,), (0,)), ((), ())), preferred_element...  1.98 us
    all_gather x1, blocking collectives, body(): lax.all_gather(scaled, 'narrow', axis=1, tiled=True)  1.9 us
  transfers between devices with their start and end apart: 13, of which 7 were waited for; matrix products, arithmetic and copies ran while one was open for 13% of the time, Pallas kernels for 0%

commit v1 on v0

v1 whole, which is shorter than its diff:
```python
import functools
import math

import jax
import jax.numpy as jnp
from jax import lax
from jax.experimental import pallas as pl
from jax.experimental.pallas import tpu as pltpu
from jax.sharding import PartitionSpec as P

LOG2E = math.log2(math.e)
NT = (((1,), (1,)), ((), ()))
TN = (((0,), (0,)), ((), ()))


def three_parts(value):
    high = value.astype(jnp.bfloat16).astype(jnp.float32)
    rest = value - high
    middle = rest.astype(jnp.bfloat16).astype(jnp.float32)
    return high, middle, rest - middle


def flipped(index, mask, bits):
    for b in range(bits):
        p = 2**b
        index = index + ((mask // p) % 2) * p * (1 - 2 * ((index // p) % 2))
    return index


def kernel(wide, points_ref, probes_ref, length_ref, out_ref, held, own, visit, pad, acc,
           send_sem, recv_sem):
    t, w, c = lax.axis_index("trial"), lax.axis_index("wide"), lax.axis_index("narrow")
    feats, pts = points_ref.shape
    cols = probes_ref.shape[0]
    lines = wide // 2
    bits = lines.bit_length() - 1
    z, y = w // 2, w % 2

    def place(j, side):
        return flipped(z, j, bits) * 2 + y + side * (1 - 2 * y)

    across = place(0, 1)
    barrier = pltpu.get_barrier_semaphore()
    peers = [(t, w, 1 - c), (t, across, c)] + [(t, place(j, 0), c) for j in range(1, lines)]
    for peer in peers:
        pl.semaphore_signal(barrier, inc=1, device_id=peer, device_id_type=pl.DeviceIdType.MESH)

    mine = held.at[w * 2 + c]
    scaled = (points_ref[...] / length_ref[...]).astype(jnp.bfloat16)
    wide_f = scaled.astype(jnp.float32)
    norm = jnp.sum(wide_f * wide_f, axis=0, keepdims=True)
    n_parts = three_parts((-0.5 * LOG2E) * norm)
    pad[...] = jnp.zeros_like(pad)
    pad[:cols] = probes_ref[...].astype(jnp.float32)
    row = lax.broadcasted_iota(jnp.int32, (32, pts), 0)
    tail = pad[...]
    mirror = jnp.zeros((32, pts), jnp.float32)
    for k, part in enumerate(n_parts):
        tail = jnp.where(row == cols + k, part, tail)
        tail = jnp.where(row == cols + 3 + k, 1.0, tail)
        mirror = jnp.where(row == cols + k, 1.0, mirror)
        mirror = jnp.where(row == cols + 3 + k, part, mirror)
    mine[:feats] = scaled
    mine[feats:] = tail.astype(jnp.bfloat16)

    pl.semaphore_wait(barrier, len(peers))

    def copy(slot, kind, device):
        return pltpu.make_async_remote_copy(
            src_ref=held.at[slot], dst_ref=held.at[slot],
            send_sem=send_sem.at[kind], recv_sem=recv_sem.at[slot],
            device_id=device, device_id_type=pl.DeviceIdType.MESH)

    def arrived(slot):
        copy(slot, 0, (t, w, c)).wait_recv()

    def to_sibling(o):
        return copy(place(o // 2, o % 2) * 2 + c, o, (t, w, 1 - c))

    def to_across(j):
        return copy(place(j, 0) * 2 + c, wide + j, (t, across, c))

    def along(j):
        return copy(w * 2 + c, wide + lines + j, (t, place(j, 0), c))

    to_across(0).start()
    to_sibling(0).start()
    for j in range(1, lines):
        along(j).start()

    for k, part in enumerate(three_parts(wide_f * LOG2E)):
        own[feats * k:feats * (k + 1)] = part.astype(jnp.bfloat16)
    own[3 * feats:] = mirror.astype(jnp.bfloat16)
    acc[...] = jnp.zeros_like(acc)

    def step(s, _):
        o, half = s // 2, s % 2
        slot = place(o // 2, o % 2) * 2 + c + half * (1 - 2 * c)

        @pl.when((half == 0) & (o % 2 == 1))
        def _():
            arrived(slot)
            to_sibling(o).start()

        @pl.when(half == 1)
        def _():
            arrived(slot)

            @pl.when((o % 2 == 1) & (o + 1 < wide))
            def _():
                j = (o + 1) // 2
                arrived(place(j, 0) * 2 + c)
                to_across(j).start()
                to_sibling(o + 1).start()

        block = held.at[slot]
        for k in range(3):
            visit[feats * k:feats * (k + 1)] = block[:feats]
        visit[3 * feats:] = block[feats:]
        cross = lax.dot_general(visit[...], own[...], TN, preferred_element_type=jnp.float32)
        tile = jnp.exp2(cross).astype(jnp.bfloat16)
        acc[...] += jnp.dot(block[feats:], tile, preferred_element_type=jnp.float32)
        return 0

    lax.fori_loop(0, 2 * wide, step, 0)
    out_ref[...] = acc[:cols]

    for o in range(wide):
        to_sibling(o).wait_send()
    for j in range(lines):
        to_across(j).wait_send()
    for j in range(1, lines):
        along(j).wait_send()


def solution(mesh):
    wide = mesh.shape["wide"]

    def body(points, probes, lengthscale, noise):
        feats, pts = points.shape
        cols = probes.shape[0]
        rows = feats + 32
        summed = pl.pallas_call(
            functools.partial(kernel, wide),
            out_shape=jax.ShapeDtypeStruct((cols, pts), jnp.float32),
            in_specs=[pl.BlockSpec(memory_space=pltpu.VMEM)] * 3,
            out_specs=pl.BlockSpec(memory_space=pltpu.VMEM),
            scratch_shapes=[
                pltpu.VMEM((2 * wide, rows, pts), jnp.bfloat16),
                pltpu.VMEM((3 * feats + 32, pts), jnp.bfloat16),
                pltpu.VMEM((3 * feats + 32, pts), jnp.bfloat16),
                pltpu.VMEM((32, pts), jnp.float32),
                pltpu.VMEM((32, pts), jnp.float32),
                pltpu.SemaphoreType.DMA((2 * wide,)),
                pltpu.SemaphoreType.DMA((2 * wide,)),
            ],
            compiler_params=pltpu.CompilerParams(
                collective_id=0, has_side_effects=True, vmem_limit_bytes=40 * 2**20),
        )(points, probes, lengthscale[:, None])
        return summed + noise[0] * probes.astype(jnp.float32)

    placed = (
        P(None, ("trial", "wide", "narrow")),
        P(None, ("trial", "wide", "narrow")),
        P("trial"),
        P("trial"),
    )
    return jax.shard_map(
        body, mesh=mesh, in_specs=placed,
        out_specs=P(None, ("trial", "wide", "narrow")), check_vma=False)
```

time: 78.5 us -> 34.9 us (0.44)
  Pallas kernels: 0 us -> 31 us
  waiting for transfers between devices: 28.8 us -> 0 us
  matrix products: 19.2 us -> 0 us
  between operations: 14.1 us -> 0.66 us
  starting transfers between devices: 8.97 us -> 0 us
  blocking collectives: 4.25 us -> 0 us
  local copies, waits for them, and re-layouts: 0.04 us -> 2.44 us
  other arithmetic: 2.72 us -> 0.66 us
    pallas_call x0 -> x1, Pallas kernels: none -> 31 us  [body(): pl.pallas_call(functools.partial(kernel, wide), out_shape=jax.ShapeDtypeS...]
    ppermute x12 -> x0, waiting for transfers between devices: 28.6 us -> none  [passed_along(): return lax.ppermute(block, axis, route)]
    dot_general x11 -> x0, matrix products: 19.2 us -> none  [the longest x5 10.7 us: row_term(): lax.dot_general(cols_v, tile, (((1,), (1,)), ((), ())), preferred_element...]
    ppermute x12 -> x0, starting transfers between devices: 8.96 us -> none  [passed_along(): return lax.ppermute(block, axis, route)]
    all_gather x2 -> x0, blocking collectives: 4.25 us -> none  [the longest x1 2.34 us: body(): lax.all_gather(probes, 'narrow', axis=1, tiled=True)]
    unnamed x4 -> x6, local copies, waits for them, and re-layouts: 0.01 us -> 2.36 us
    reduce_sum x6 -> x0, other arithmetic: 1.14 us -> none  [the longest x5 1.1 us: kernel_tile(): cols_n = jnp.sum(cols_f * cols_f, axis=0)]
    add x1, other arithmetic: 1.55 us -> 0.66 us  [body(): return summed + noise[0] * probes.astype(jnp.float32)]
  transfers between devices with their start and end apart: 13 -> 0, of which waited for: 7 -> 0; matrix products, arithmetic and copies ran while one was open for 13% -> 0% of each run, Pallas kernels for 0% -> 0%
where the time goes in v1:
time: 34.9 us; the launch traced here: 34.7 us
  Pallas kernels  31 us (89%)
  local copies, waits for them, and re-layouts  2.44 us (7%)
  other arithmetic  0.66 us (2%)
  between operations  0.66 us (2%)
    pallas_call x1, Pallas kernels, body(): pl.pallas_call(functools.partial(kernel, wide), out_shape=jax.ShapeDtypeS...  31 us
    unnamed x6, local copies, waits for them, and re-layouts  2.36 us

profile of v1, /device:TPU:0, one launch (start us, length us, event | category | flops | bytes accessed | tf_op | source)
XLA Modules:
  0.0 34.7 jit_solution(7006428033978374216)
XLA Ops:
  0.0 0.0 copy-start.2
  0.0 0.7 %copy-done.2 = f32[32]{0:T(128)S(1)} copy-done((f32[32]{0:T(128)S(1)}, f32[32]{0:T(128)}, u32[]{:S(2)}) %copy-start.2) | copy-done | bytes 152
  0.7 0.1 copy.5.length_ref
  0.7 0.0 copy-start
  0.7 0.8 %copy-done = bf16[17,1024]{1,0:T(8,128)(2,1)S(1)} copy-done((bf16[17,1024]{1,0:T(8,128)(2,1)S(1)}, bf16[17,1024]{1,0:T(8,128)(2,1)}, u32[]{:S(2)}) %copy-start) | copy-done | bytes 34840
  1.5 0.0 copy-start.1
  1.5 0.9 %copy-done.1 = f32[32,1024]{1,0:T(8,128)S(1)} copy-done((f32[32,1024]{1,0:T(8,128)S(1)}, f32[32,1024]{1,0:T(8,128)}, u32[]{:S(2)}) %copy-start.1) | copy-done | bytes 131096
  2.4 31.0 %shard_map.46 = f32[17,1024]{1,0:T(8,128)S(1)} custom-call(f32[32,1024]{1,0:T(8,128)S(1)} %copy-done.1, bf16[17,1024]{1,0:T(8,128)(2,1)S(1)} %copy-done, f32[32,1]{1,0:T(8,128)S(1)} %copy.5.length_ref), custom_call_target="tpu_custom_call" | custom-call | tf_op jit(solution)/shard_map/pallas_call | solution.py:143
  34.1 0.7 %multiply_add_fusion = f32[17,1024]{1,0:T(8,128)} fusion(f32[17,1024]{1,0:T(8,128)S(1)} %shard_map.46, bf16[17,1024]{1,0:T(8,128)(2,1)S(1)} %copy-done, f32[]{:T(128)} %bitcast.2), kind=kLoop, calls=%fused_computation | loop fusion | flops 52224 | bytes 174084 | tf_op jit(solution)/shard_map/add | solution.py:160
Async XLA Ops:
  0.0 0.7 %copy-start.2 = (f32[32]{0:T(128)S(1)}, f32[32]{0:T(128)}, u32[]{:S(2)}) copy-start(f32[32]{0:T(128)} %param.6) | copy-start | bytes 388
  0.7 0.8 %copy-start = (bf16[17,1024]{1,0:T(8,128)(2,1)S(1)}, bf16[17,1024]{1,0:T(8,128)(2,1)}, u32[]{:S(2)}) copy-start(bf16[17,1024]{1,0:T(8,128)(2,1)} %probes_ref.1) | copy-start | bytes 104452
  1.5 0.9 %copy-start.1 = (f32[32,1024]{1,0:T(8,128)S(1)}, f32[32,1024]{1,0:T(8,128)}, u32[]{:S(2)}) copy-start(f32[32,1024]{1,0:T(8,128)} %points_ref.1) | copy-start | bytes 393220

commit v2 on v1

--- a/solution.py
+++ b/solution.py
@@ -27,8 +27,12 @@
     return index
 
 
-def kernel(wide, points_ref, probes_ref, length_ref, out_ref, held, own, visit, pad, acc,
-           send_sem, recv_sem):
+def kernel(wide, points_hbm, probes_hbm, length_hbm, out_ref, held, own, visit, pad, acc,
+           points_ref, probes_ref, length_ref, load_sem, send_sem, recv_sem):
+    loads = [pltpu.make_async_copy(a, b, load_sem.at[i]) for i, (a, b) in enumerate(
+        [(points_hbm, points_ref), (probes_hbm, probes_ref), (length_hbm, length_ref)])]
+    for load in loads:
+        load.start()
     t, w, c = lax.axis_index("trial"), lax.axis_index("wide"), lax.axis_index("narrow")
     feats, pts = points_ref.shape
     cols = probes_ref.shape[0]
@@ -45,6 +49,8 @@
     for peer in peers:
         pl.semaphore_signal(barrier, inc=1, device_id=peer, device_id_type=pl.DeviceIdType.MESH)
 
+    for load in loads:
+        load.wait()
     mine = held.at[w * 2 + c]
     scaled = (points_ref[...] / length_ref[...]).astype(jnp.bfloat16)
     wide_f = scaled.astype(jnp.float32)
@@ -74,8 +80,16 @@
     def arrived(slot):
         copy(slot, 0, (t, w, c)).wait_recv()
 
-    def to_sibling(o):
-        return copy(place(o // 2, o % 2) * 2 + c, o, (t, w, 1 - c))
+    def item(k):
+        odd, later, last = k % 2, (k + wide - 1) // wide, (k + 1) // wide
+        j = odd * ((k + 1) // 2 - last) + (1 - odd) * (k // 2 - later)
+        return j, odd * last + (1 - odd) * later
+
+    def slot_of(k):
+        return place(*item(k)) * 2 + c
+
+    def to_sibling(k):
+        return copy(slot_of(k), k, (t, w, 1 - c))
 
     def to_across(j):
         return copy(place(j, 0) * 2 + c, wide + j, (t, across, c))
@@ -84,34 +98,41 @@
         return copy(w * 2 + c, wide + lines + j, (t, place(j, 0), c))
 
     to_across(0).start()
-    to_sibling(0).start()
     for j in range(1, lines):
         along(j).start()
+    to_sibling(0).start()
 
     for k, part in enumerate(three_parts(wide_f * LOG2E)):
         own[feats * k:feats * (k + 1)] = part.astype(jnp.bfloat16)
     own[3 * feats:] = mirror.astype(jnp.bfloat16)
     acc[...] = jnp.zeros_like(acc)
 
+    def forward(k):
+        j, side = item(k)
+        arrived(slot_of(k))
+
+        @pl.when(side == 0)
+        def _():
+            to_across(j).start()
+
+        to_sibling(k).start()
+
     def step(s, _):
         o, half = s // 2, s % 2
-        slot = place(o // 2, o % 2) * 2 + c + half * (1 - 2 * c)
+        slot = slot_of(o) + half * (1 - 2 * c)
 
-        @pl.when((half == 0) & (o % 2 == 1))
+        @pl.when(s == 2)
         def _():
-            arrived(slot)
-            to_sibling(o).start()
+            forward(1)
+            forward(2)
 
         @pl.when(half == 1)
         def _():
             arrived(slot)
 
-            @pl.when((o % 2 == 1) & (o + 1 < wide))
+            @pl.when((o >= 2) & (o + 1 < wide))
             def _():
-                j = (o + 1) // 2
-                arrived(place(j, 0) * 2 + c)
-                to_across(j).start()
-                to_sibling(o + 1).start()
+                forward(o + 1)
 
         block = held.at[slot]
         for k in range(3):
@@ -143,7 +164,7 @@
         summed = pl.pallas_call(
             functools.partial(kernel, wide),
             out_shape=jax.ShapeDtypeStruct((cols, pts), jnp.float32),
-            in_specs=[pl.BlockSpec(memory_space=pltpu.VMEM)] * 3,
+            in_specs=[pl.BlockSpec(memory_space=pltpu.HBM)] * 3,
             out_specs=pl.BlockSpec(memory_space=pltpu.VMEM),
             scratch_shapes=[
                 pltpu.VMEM((2 * wide, rows, pts), jnp.bfloat16),
@@ -151,6 +172,10 @@
                 pltpu.VMEM((3 * feats + 32, pts), jnp.bfloat16),
                 pltpu.VMEM((32, pts), jnp.float32),
                 pltpu.VMEM((32, pts), jnp.float32),
+                pltpu.VMEM((feats, pts), points.dtype),
+                pltpu.VMEM((cols, pts), probes.dtype),
+                pltpu.VMEM((feats, 1), lengthscale.dtype),
+                pltpu.SemaphoreType.DMA((3,)),
                 pltpu.SemaphoreType.DMA((2 * wide,)),
                 pltpu.SemaphoreType.DMA((2 * wide,)),
             ],

time: 34.9 us -> 32.1 us (0.920)
  Pallas kernels: 31 us -> 28.2 us
    pallas_call x1, Pallas kernels: 31 us -> 28.2 us  [body(): pl.pallas_call(functools.partial(kernel, wide), out_shape=jax.ShapeDtypeS...]
where the time goes in v2:
time: 32.1 us; the launch traced here: 31.9 us
  Pallas kernels  28.2 us (88%)
  local copies, waits for them, and re-layouts  2.44 us (8%)
  other arithmetic  0.66 us (2%)
  between operations  0.66 us (2%)
    pallas_call x1, Pallas kernels, body(): pl.pallas_call(functools.partial(kernel, wide), out_shape=jax.ShapeDtypeS...  28.2 us
    unnamed x6, local copies, waits for them, and re-layouts  2.36 us
    add x1, other arithmetic, body(): return summed + noise[0] * probes.astype(jnp.float32)  0.66 us

profile of v2, /device:TPU:0, one launch (start us, length us, event | category | flops | bytes accessed | tf_op | source)
XLA Modules:
  0.0 31.9 jit_solution(2624845596508271343)
XLA Ops:
  0.0 0.0 copy-start.2
  0.0 0.7 %copy-done.2 = f32[32]{0:T(128)S(1)} copy-done((f32[32]{0:T(128)S(1)}, f32[32]{0:T(128)}, u32[]{:S(2)}) %copy-start.2) | copy-done | bytes 152
  0.7 0.1 copy.5.length_hbm
  0.7 0.0 copy-start
  0.7 0.8 %copy-done = bf16[17,1024]{1,0:T(8,128)(2,1)S(1)} copy-done((bf16[17,1024]{1,0:T(8,128)(2,1)S(1)}, bf16[17,1024]{1,0:T(8,128)(2,1)}, u32[]{:S(2)}) %copy-start) | copy-done | bytes 34840
  1.5 0.0 copy-start.1
  1.5 0.9 %copy-done.1 = f32[32,1024]{1,0:T(8,128)S(1)} copy-done((f32[32,1024]{1,0:T(8,128)S(1)}, f32[32,1024]{1,0:T(8,128)}, u32[]{:S(2)}) %copy-start.1) | copy-done | bytes 131096
  2.4 28.2 %shard_map.46 = f32[17,1024]{1,0:T(8,128)S(1)} custom-call(f32[32,1024]{1,0:T(8,128)S(1)} %copy-done.1, bf16[17,1024]{1,0:T(8,128)(2,1)S(1)} %copy-done, f32[32,1]{1,0:T(8,128)S(1)} %copy.5.length_hbm), custom_call_target="tpu_custom_call" | custom-call | tf_op jit(solution)/shard_map/pallas_call | solution.py:164
  31.3 0.7 %multiply_add_fusion = f32[17,1024]{1,0:T(8,128)} fusion(f32[17,1024]{1,0:T(8,128)S(1)} %shard_map.46, bf16[17,1024]{1,0:T(8,128)(2,1)S(1)} %copy-done, f32[]{:T(128)} %bitcast.2), kind=kLoop, calls=%fused_computation | loop fusion | flops 52224 | bytes 174084 | tf_op jit(solution)/shard_map/add | solution.py:185
Async XLA Ops:
  0.0 0.7 %copy-start.2 = (f32[32]{0:T(128)S(1)}, f32[32]{0:T(128)}, u32[]{:S(2)}) copy-start(f32[32]{0:T(128)} %param.6) | copy-start | bytes 388
  0.7 0.8 %copy-start = (bf16[17,1024]{1,0:T(8,128)(2,1)S(1)}, bf16[17,1024]{1,0:T(8,128)(2,1)}, u32[]{:S(2)}) copy-start(bf16[17,1024]{1,0:T(8,128)(2,1)} %probes_hbm.1) | copy-start | bytes 104452
  1.5 0.9 %copy-start.1 = (f32[32,1024]{1,0:T(8,128)S(1)}, f32[32,1024]{1,0:T(8,128)}, u32[]{:S(2)}) copy-start(f32[32,1024]{1,0:T(8,128)} %points_hbm.1) | copy-start | bytes 393220

commit v3 on v2

--- a/solution.py
+++ b/solution.py
@@ -20,15 +20,9 @@
     return high, middle, rest - middle
 
 
-def flipped(index, mask, bits):
-    for b in range(bits):
-        p = 2**b
-        index = index + ((mask // p) % 2) * p * (1 - 2 * ((index // p) % 2))
-    return index
-
-
 def kernel(wide, points_hbm, probes_hbm, length_hbm, out_ref, held, own, visit, pad, acc,
-           points_ref, probes_ref, length_ref, load_sem, send_sem, recv_sem):
+           points_ref, probes_ref, length_ref, load_sem, sib_sem, side_sem, up_sem, down_sem,
+           recv_sem):
     loads = [pltpu.make_async_copy(a, b, load_sem.at[i]) for i, (a, b) in enumerate(
         [(points_hbm, points_ref), (probes_hbm, probes_ref), (length_hbm, length_ref)])]
     for load in loads:
@@ -37,17 +31,31 @@
     feats, pts = points_ref.shape
     cols = probes_ref.shape[0]
     lines = wide // 2
-    bits = lines.bit_length() - 1
     z, y = w // 2, w % 2
-
-    def place(j, side):
-        return flipped(z, j, bits) * 2 + y + side * (1 - 2 * y)
-
-    across = place(0, 1)
+    upper = z * 2 // lines
+    paired = z * (1 - upper) + (lines - 1 - z) * upper
+    far = 4 * lines
+
+    def at_rank(r):
+        lone = (r + far - 2 * paired - 1) // far
+        step = (1 - lone) * ((r + 1) // 2) * (2 * ((r + 1) % 2) - 1) + lone * (r - paired) * (1 - 2 * upper)
+        return z + step
+
+    def place(line, side):
+        return line * 2 + y + side * (1 - 2 * y)
+
+    across = place(z, 1)
     barrier = pltpu.get_barrier_semaphore()
-    peers = [(t, w, 1 - c), (t, across, c)] + [(t, place(j, 0), c) for j in range(1, lines)]
-    for peer in peers:
+    for peer in [(t, w, 1 - c), (t, across, c)]:
         pl.semaphore_signal(barrier, inc=1, device_id=peer, device_id_type=pl.DeviceIdType.MESH)
+
+    @pl.when(z > 0)
+    def _():
+        pl.semaphore_signal(barrier, inc=1, device_id=(t, w - 2, c), device_id_type=pl.DeviceIdType.MESH)
+
+    @pl.when(z < lines - 1)
+    def _():
+        pl.semaphore_signal(barrier, inc=1, device_id=(t, w + 2, c), device_id_type=pl.DeviceIdType.MESH)
 
     for load in loads:
         load.wait()
@@ -69,70 +77,112 @@
     mine[:feats] = scaled
     mine[feats:] = tail.astype(jnp.bfloat16)
 
-    pl.semaphore_wait(barrier, len(peers))
-
-    def copy(slot, kind, device):
+    ends = (z + lines - 1) // lines + (2 * lines - 2 - z) // lines
+    pl.semaphore_wait(barrier, 2 + ends)
+
+    def copy(where, half, sems, device):
+        rows = pl.ds(half * feats, feats if half == 0 else 32)
         return pltpu.make_async_remote_copy(
-            src_ref=held.at[slot], dst_ref=held.at[slot],
-            send_sem=send_sem.at[kind], recv_sem=recv_sem.at[slot],
+            src_ref=held.at[where * 2 + c, rows], dst_ref=held.at[where * 2 + c, rows],
+            send_sem=sems.at[where * 2 + half], recv_sem=recv_sem.at[(where * 2 + c) * 2 + half],
             device_id=device, device_id_type=pl.DeviceIdType.MESH)
 
-    def arrived(slot):
-        copy(slot, 0, (t, w, c)).wait_recv()
-
-    def item(k):
-        odd, later, last = k % 2, (k + wide - 1) // wide, (k + 1) // wide
-        j = odd * ((k + 1) // 2 - last) + (1 - odd) * (k // 2 - later)
-        return j, odd * last + (1 - odd) * later
-
-    def slot_of(k):
-        return place(*item(k)) * 2 + c
-
-    def to_sibling(k):
-        return copy(slot_of(k), k, (t, w, 1 - c))
-
-    def to_across(j):
-        return copy(place(j, 0) * 2 + c, wide + j, (t, across, c))
-
-    def along(j):
-        return copy(w * 2 + c, wide + lines + j, (t, place(j, 0), c))
-
-    to_across(0).start()
-    for j in range(1, lines):
-        along(j).start()
-    to_sibling(0).start()
+    def arrived(slot, half):
+        rows = pl.ds(half * feats, feats if half == 0 else 32)
+        pltpu.make_async_remote_copy(
+            src_ref=held.at[slot, rows], dst_ref=held.at[slot, rows],
+            send_sem=sib_sem.at[half], recv_sem=recv_sem.at[slot * 2 + half],
+            device_id=(t, w, 1 - c), device_id_type=pl.DeviceIdType.MESH).wait_recv()
+
+    def to_sibling(where, half):
+        return copy(where, half, sib_sem, (t, w, 1 - c))
+
+    def to_across(where, half):
+        return copy(where, half, side_sem, (t, across, c))
+
+    def upward(where, half):
+        return copy(where, half, up_sem, (t, w + 2, c))
+
+    def downward(where, half):
+        return copy(where, half, down_sem, (t, w - 2, c))
+
+    for half in range(2):
+        to_across(w, half).start()
+
+        @pl.when(z < lines - 1)
+        def _():
+            upward(w, half).start()
+
+        @pl.when(z > 0)
+        def _():
+            downward(w, half).start()
+
+        to_sibling(w, half).start()
 
     for k, part in enumerate(three_parts(wide_f * LOG2E)):
         own[feats * k:feats * (k + 1)] = part.astype(jnp.bfloat16)
     own[3 * feats:] = mirror.astype(jnp.bfloat16)
     acc[...] = jnp.zeros_like(acc)
 
-    def forward(k):
-        j, side = item(k)
-        arrived(slot_of(k))
-
-        @pl.when(side == 0)
-        def _():
-            to_across(j).start()
-
-        to_sibling(k).start()
+    def from_line(d, half):
+        @pl.when(z - d >= 0)
+        def _():
+            below = w - 2 * d
+            arrived(below * 2 + c, half)
+
+            @pl.when(z < lines - 1)
+            def _():
+                upward(below, half).start()
+
+            to_across(below, half).start()
+            to_sibling(below, half).start()
+
+        @pl.when(z + d < lines)
+        def _():
+            above = w + 2 * d
+            arrived(above * 2 + c, half)
+
+            @pl.when(z > 0)
+            def _():
+                downward(above, half).start()
+
+            to_across(above, half).start()
+            to_sibling(above, half).start()
+
+    def where_of(k):
+        odd, later, last = k % 2, (k + wide - 1) // wide, (k + 1) // wide
+        rank = odd * ((k + 1) // 2 - last) + (1 - odd) * (k // 2 - later)
+        return place(at_rank(rank), odd * last + (1 - odd) * later)
 
     def step(s, _):
         o, half = s // 2, s % 2
-        slot = slot_of(o) + half * (1 - 2 * c)
+        slot = where_of(o) * 2 + c + half * (1 - 2 * c)
 
         @pl.when(s == 2)
         def _():
-            forward(1)
-            forward(2)
+            from_line(1, 0)
+            from_line(1, 1)
+
+        @pl.when((s % 3 == 1) & (s >= 4))
+        def _():
+            from_line((s + 2) // 3, 0)
+
+        @pl.when((s % 3 == 2) & (s >= 5))
+        def _():
+            from_line((s + 1) // 3, 1)
 
         @pl.when(half == 1)
         def _():
-            arrived(slot)
-
-            @pl.when((o >= 2) & (o + 1 < wide))
-            def _():
-                forward(o + 1)
+            arrived(slot, 0)
+            arrived(slot, 1)
+            k = o + 1
+
+            @pl.when(((k % 2 == 0) & (k < wide)) | (k == wide - 1))
+            def _():
+                there = where_of(k)
+                for part in range(2):
+                    arrived(there * 2 + c, part)
+                    to_sibling(there, part).start()
 
         block = held.at[slot]
         for k in range(3):
@@ -146,12 +196,19 @@
     lax.fori_loop(0, 2 * wide, step, 0)
     out_ref[...] = acc[:cols]
 
-    for o in range(wide):
-        to_sibling(o).wait_send()
-    for j in range(lines):
-        to_across(j).wait_send()
-    for j in range(1, lines):
-        along(j).wait_send()
+    for half in range(2):
+        for where in range(wide):
+            to_sibling(where, half).wait_send()
+        for line in range(lines):
+            to_across(place(line, 0), half).wait_send()
+
+            @pl.when((line <= z) & (z < lines - 1))
+            def _():
+                upward(place(line, 0), half).wait_send()
+
+            @pl.when((line >= z) & (z > 0))
+            def _():
+                downward(place(line, 0), half).wait_send()
 
 
 def solution(mesh):
@@ -178,9 +235,12 @@
                 pltpu.SemaphoreType.DMA((3,)),
                 pltpu.SemaphoreType.DMA((2 * wide,)),
                 pltpu.SemaphoreType.DMA((2 * wide,)),
+                pltpu.SemaphoreType.DMA((2 * wide,)),
+                pltpu.SemaphoreType.DMA((2 * wide,)),
+                pltpu.SemaphoreType.DMA((4 * wide,)),
             ],
             compiler_params=pltpu.CompilerParams(
-                collective_id=0, has_side_effects=True, vmem_limit_bytes=40 * 2**20),
+                collective_id=0, has_side_effects=True, vmem_limit_bytes=64 * 2**20 - 2**17),
         )(points, probes, lengthscale[:, None])
         return summed + noise[0] * probes.astype(jnp.float32)
 

time: 32.1 us -> 29.8 us (0.928)
  Pallas kernels: 28.2 us -> 26.1 us
  local copies, waits for them, and re-layouts: 2.44 us -> 1.35 us
  other arithmetic: 0.66 us -> 1.55 us
    pallas_call x1, Pallas kernels: 28.2 us -> 26.1 us  [body(): pl.pallas_call(functools.partial(kernel, wide), out_shape=jax.ShapeDtypeS...]
    unnamed x6 -> x4, local copies, waits for them, and re-layouts: 2.36 us -> 0.66 us
    add x1, other arithmetic: 0.66 us -> 1.55 us  [body(): return summed + noise[0] * probes.astype(jnp.float32)]
    broadcast_in_dim x1, local copies, waits for them, and re-layouts: 0.09 us -> 0.69 us  [body(): lengthscale[:, None]]
where the time goes in v3:
time: 29.8 us; the launch traced here: 29.7 us
  Pallas kernels  26.1 us (88%)
  other arithmetic  1.55 us (5%)
  local copies, waits for them, and re-layouts  1.35 us (5%)
  between operations  0.67 us (2%)
    pallas_call x1, Pallas kernels, body(): pl.pallas_call(functools.partial(kernel, wide), out_shape=jax.ShapeDtypeS...  26.1 us
    add x1, other arithmetic, body(): return summed + noise[0] * probes.astype(jnp.float32)  1.55 us
    broadcast_in_dim x1, local copies, waits for them, and re-layouts, body(): lengthscale[:, None]  0.69 us
    unnamed x4, local copies, waits for them, and re-layouts  0.66 us

profile of v3, /device:TPU:0, one launch (start us, length us, event | category | flops | bytes accessed | tf_op | source)
XLA Modules:
  0.0 29.7 jit_solution(8598176283209503227)
XLA Ops:
  0.0 0.0 copy-start.1
  0.0 0.7 %copy-done.1 = f32[32]{0:T(128)S(1)} copy-done((f32[32]{0:T(128)S(1)}, f32[32]{0:T(128)}, u32[]{:S(2)}) %copy-start.1) | copy-done | bytes 152
  0.7 0.7 %copy.5.length_hbm = f32[32,1]{1,0:T(8,128)} copy(f32[32,1]{0,1:T(1,128)S(1)} %bitcast.3) | data formatting | bytes 256 | tf_op jit(solution)/shard_map/broadcast_in_dim | solution.py:244
  1.3 0.0 copy-start
  1.3 26.1 %shard_map.46 = f32[17,1024]{1,0:T(8,128)} custom-call(f32[32,1024]{1,0:T(8,128)} %points_hbm.1, bf16[17,1024]{1,0:T(8,128)(2,1)} %probes_hbm.1, f32[32,1]{1,0:T(8,128)} %copy.5.length_hbm), custom_call_target="tpu_custom_call" | custom-call | tf_op jit(solution)/shard_map/pallas_call | solution.py:221
  28.1 0.0 copy-done
  28.1 1.5 %multiply_add_fusion = f32[17,1024]{1,0:T(8,128)} fusion(f32[17,1024]{1,0:T(8,128)} %shard_map.46, bf16[17,1024]{1,0:T(8,128)(2,1)S(1)} %copy-done, f32[]{:T(128)} %bitcast.2), kind=kLoop, calls=%fused_computation | loop fusion | flops 52224 | bytes 174084 | tf_op jit(solution)/shard_map/add | solution.py:245
Async XLA Ops:
  0.0 0.7 %copy-start.1 = (f32[32]{0:T(128)S(1)}, f32[32]{0:T(128)}, u32[]{:S(2)}) copy-start(f32[32]{0:T(128)} %param.6) | copy-start | bytes 388
  1.3 26.7 %copy-start = (bf16[17,1024]{1,0:T(8,128)(2,1)S(1)}, bf16[17,1024]{1,0:T(8,128)(2,1)}, u32[]{:S(2)}) copy-start(bf16[17,1024]{1,0:T(8,128)(2,1)} %probes_hbm.1) | copy-start | bytes 104452

commit v4 on v3

--- a/solution.py
+++ b/solution.py
@@ -20,11 +20,12 @@
     return high, middle, rest - middle
 
 
-def kernel(wide, points_hbm, probes_hbm, length_hbm, out_ref, held, own, visit, pad, acc,
-           points_ref, probes_ref, length_ref, load_sem, sib_sem, side_sem, up_sem, down_sem,
+def kernel(wide, points_hbm, probes_hbm, length_hbm, noise_hbm, out_ref, held, own, visit, pad, acc,
+           points_ref, probes_ref, length_ref, noise_ref, load_sem, sib_sem, side_sem, up_sem, down_sem,
            recv_sem):
     loads = [pltpu.make_async_copy(a, b, load_sem.at[i]) for i, (a, b) in enumerate(
-        [(points_hbm, points_ref), (probes_hbm, probes_ref), (length_hbm, length_ref)])]
+        [(points_hbm, points_ref), (probes_hbm, probes_ref), (length_hbm, length_ref),
+         (noise_hbm, noise_ref)])]
     for load in loads:
         load.start()
     t, w, c = lax.axis_index("trial"), lax.axis_index("wide"), lax.axis_index("narrow")
@@ -60,7 +61,10 @@
     for load in loads:
         load.wait()
     mine = held.at[w * 2 + c]
-    scaled = (points_ref[...] / length_ref[...]).astype(jnp.bfloat16)
+    square = (feats, feats)
+    diagonal = lax.broadcasted_iota(jnp.int32, square, 0) == lax.broadcasted_iota(jnp.int32, square, 1)
+    length = jnp.sum(jnp.where(diagonal, length_ref[...], 0.0), axis=1, keepdims=True)
+    scaled = (points_ref[...] / length).astype(jnp.bfloat16)
     wide_f = scaled.astype(jnp.float32)
     norm = jnp.sum(wide_f * wide_f, axis=0, keepdims=True)
     n_parts = three_parts((-0.5 * LOG2E) * norm)
@@ -194,7 +198,7 @@
         return 0
 
     lax.fori_loop(0, 2 * wide, step, 0)
-    out_ref[...] = acc[:cols]
+    out_ref[...] = acc[:cols] + noise_ref[...] * pad[:cols]
 
     for half in range(2):
         for where in range(wide):
@@ -218,10 +222,10 @@
         feats, pts = points.shape
         cols = probes.shape[0]
         rows = feats + 32
-        summed = pl.pallas_call(
+        return pl.pallas_call(
             functools.partial(kernel, wide),
             out_shape=jax.ShapeDtypeStruct((cols, pts), jnp.float32),
-            in_specs=[pl.BlockSpec(memory_space=pltpu.HBM)] * 3,
+            in_specs=[pl.BlockSpec(memory_space=pltpu.HBM)] * 4,
             out_specs=pl.BlockSpec(memory_space=pltpu.VMEM),
             scratch_shapes=[
                 pltpu.VMEM((2 * wide, rows, pts), jnp.bfloat16),
@@ -231,8 +235,9 @@
                 pltpu.VMEM((32, pts), jnp.float32),
                 pltpu.VMEM((feats, pts), points.dtype),
                 pltpu.VMEM((cols, pts), probes.dtype),
-                pltpu.VMEM((feats, 1), lengthscale.dtype),
-                pltpu.SemaphoreType.DMA((3,)),
+                pltpu.VMEM((1, feats), lengthscale.dtype),
+                pltpu.VMEM((1, 1), noise.dtype),
+                pltpu.SemaphoreType.DMA((4,)),
                 pltpu.SemaphoreType.DMA((2 * wide,)),
                 pltpu.SemaphoreType.DMA((2 * wide,)),
                 pltpu.SemaphoreType.DMA((2 * wide,)),
@@ -241,8 +246,7 @@
             ],
             compiler_params=pltpu.CompilerParams(
                 collective_id=0, has_side_effects=True, vmem_limit_bytes=64 * 2**20 - 2**17),
-        )(points, probes, lengthscale[:, None])
-        return summed + noise[0] * probes.astype(jnp.float32)
+        )(points, probes, lengthscale[None], noise[None])
 
     placed = (
         P(None, ("trial", "wide", "narrow")),

time: 29.8 us -> 28.5 us (0.956)
  other arithmetic: 1.55 us -> 0 us
    add x1 -> x0, other arithmetic: 1.55 us -> none  [body(): return summed + noise[0] * probes.astype(jnp.float32)]
    unnamed x4 -> x1, local copies, waits for them, and re-layouts: 0.66 us -> 1.54 us
    broadcast_in_dim x1 -> x0, local copies, waits for them, and re-layouts: 0.69 us -> none  [body(): lengthscale[:, None]]
where the time goes in v4:
time: 28.5 us; the launch traced here: 28.4 us
  Pallas kernels  26.2 us (92%)
  local copies, waits for them, and re-layouts  1.54 us (5%)
  between operations  0.66 us (2%)
    pallas_call x1, Pallas kernels, body(): pl.pallas_call(functools.partial(kernel, wide), out_shape=jax.ShapeDtypeS...  26.2 us
    unnamed x1, local copies, waits for them, and re-layouts  1.54 us

profile of v4, /device:TPU:0, one launch (start us, length us, event | category | flops | bytes accessed | tf_op | source)
XLA Modules:
  0.0 28.4 jit_solution(1240967528095587512)
XLA Ops:
  0.7 26.2 %shard_map.46 = f32[17,1024]{1,0:T(8,128)} custom-call(f32[32,1024]{1,0:T(8,128)} %points_hbm.1, bf16[17,1024]{1,0:T(8,128)(2,1)} %probes_hbm.1, f32[1,32]{1,0:T(1,128)} %bitcast.3, f32[1,1]{1,0:T(1,128)} %bitcast.2.noise_hbm), custom_call_target="tpu_custom_call" | custom-call | tf_op jit(solution)/shard_map/pallas_call | solution.py:225
  26.8 1.5 %copy.7 = f32[17,1024]{1,0:T(8,128)} copy(f32[17,1024]{1,0:T(8,128)} %shard_map.46) | data formatting | bytes 139264

commit v5 on v4

--- a/solution.py
+++ b/solution.py
@@ -167,13 +167,13 @@
             from_line(1, 0)
             from_line(1, 1)
 
-        @pl.when((s % 3 == 1) & (s >= 4))
-        def _():
-            from_line((s + 2) // 3, 0)
-
         @pl.when((s % 3 == 2) & (s >= 5))
         def _():
-            from_line((s + 1) // 3, 1)
+            from_line((s + 1) // 3, 0)
+
+        @pl.when((s % 3 == 0) & (s >= 6))
+        def _():
+            from_line(s // 3, 1)
 
         @pl.when(half == 1)
         def _():

time: 28.5 us -> 28.3 us (level)
  Pallas kernels: 26.2 us -> 25.9 us
where the time goes in v5:
time: 28.3 us; the launch traced here: 28.1 us
  Pallas kernels  25.9 us (92%)
  local copies, waits for them, and re-layouts  1.54 us (5%)
  between operations  0.66 us (2%)
    pallas_call x1, Pallas kernels, body(): pl.pallas_call(functools.partial(kernel, wide), out_shape=jax.ShapeDtypeS...  25.9 us
    unnamed x1, local copies, waits for them, and re-layouts  1.54 us

profile of v5, /device:TPU:0, one launch (start us, length us, event | category | flops | bytes accessed | tf_op | source)
XLA Modules:
  0.0 28.1 jit_solution(2955793023380211864)
XLA Ops:
  0.7 25.9 %shard_map.46 = f32[17,1024]{1,0:T(8,128)} custom-call(f32[32,1024]{1,0:T(8,128)} %points_hbm.1, bf16[17,1024]{1,0:T(8,128)(2,1)} %probes_hbm.1, f32[1,32]{1,0:T(1,128)} %bitcast.3, f32[1,1]{1,0:T(1,128)} %bitcast.2.noise_hbm), custom_call_target="tpu_custom_call" | custom-call | tf_op jit(solution)/shard_map/pallas_call | solution.py:225
  26.6 1.5 %copy.7 = f32[17,1024]{1,0:T(8,128)} copy(f32[17,1024]{1,0:T(8,128)} %shard_map.46) | data formatting | bytes 139264
